TPU v7x, 32 devices: a whole 2x2x4 slice. The times are simulated.
32 devices in a mesh: groups: 2 (over y), date: 4 (over z), pix: 2 (over x), chan: 2 (over core).
Axes of the slice: x: 2, y: 2, z: 4, core: 2. Of those that a mesh axis runs over, the one named last changes fastest.
Arguments:
- frames: bfloat16 [128, 4, 64, 128], P(('groups', 'date'), 'pix'), parts along dimension 0, may hold values from -6 to 6
- spatial_weight: bfloat16 [3, 3, 64, 64], P(None, None, None, 'chan'), may hold values from -0.25 to 0.25
- spatial_bias: float32 [64], P('chan'), may hold values from -3 to 3
- temporal_weight: bfloat16 [64, 64, 16], P('date', 'chan'), may hold values from -0.1875 to 0.1875
- temporal_bias: float32 [16], replicated, may hold values from -4 to 4
- head_weight: float32 [16], replicated, may hold values from -3 to 3
- labels: int32 [8, 128], P(('groups', 'pix'), ('date', 'chan')), parts along dimension 0, may hold values 0 or 1
Outputs:
- logits: float32 [8, 128], P(('groups', 'pix'), ('date', 'chan')), parts along dimension 0
- grad_spatial: float32 [6, 3, 64, 64], P('groups', None, None, 'chan'), parts along dimension 0
- grad_temporal: float32 [64, 64, 32], P('date', 'chan', 'groups'), parts along dimension 2
There are 2 independent parts, one for each index of `groups`. A program takes and returns all parts, laid end to end along the dimension named above; an argument that names none is the same for every part. Nothing has to cross between parts.
All inputs are finite; a program needn't handle non-finite values. No bound on the sum of `labels` on one device may be relied on, other than what follows from the above.
Results may differ from a plain program's by a relative error of at most 0.024.
Values may be sent and summed in bfloat16 or wider, within the bound.
A program may use at most 64 MiB of HBM per device.

v0:
```python
import jax
import jax.numpy as jnp
from jax import lax
from jax.sharding import PartitionSpec as P


def with_halo(block, sides, width):
    for axis, dim in sides:
        count = lax.axis_size(axis)
        forward = [(i, i + 1) for i in range(count - 1)]
        backward = [(target, source) for source, target in forward]
        low = lax.ppermute(
            lax.slice_in_dim(block, block.shape[dim] - width, None, axis=dim), axis, forward
        )
        high = lax.ppermute(lax.slice_in_dim(block, 0, width, axis=dim), axis, backward)
        block = jnp.concatenate([low, block, high], axis=dim)
    return block


def shards(
    frames, spatial_weight, spatial_bias, temporal_weight, temporal_bias, head_weight, labels
):
    dates_here, rows, channels, columns = frames.shape
    padded = with_halo(frames, (("pix", 1),), 1)
    padded = jnp.pad(padded, ((0, 0), (0, 0), (0, 0), (1, 1)))
    preact = spatial_bias[None, None, :, None]
    for row_off in range(3):
        for col_off in range(3):
            window = padded[:, row_off : row_off + rows, :, col_off : col_off + columns]
            preact = preact + jnp.einsum(
                "ticj,co->tioj",
                window,
                spatial_weight[row_off, col_off],
                preferred_element_type=jnp.float32,
            )
    sigmoid_pre = jax.nn.sigmoid(preact)
    hidden = (preact * sigmoid_pre).astype(jnp.bfloat16)
    partial_feat = jnp.einsum(
        "tioj,tof->fij", hidden, temporal_weight, preferred_element_type=jnp.float32
    )
    feature = (
        lax.psum_scatter(partial_feat, ("date", "chan"), scatter_dimension=2, tiled=True)
        + temporal_bias[:, None, None]
    )
    sigmoid_feat = jax.nn.sigmoid(feature)
    logits = jnp.einsum("fij,f->ij", feature * sigmoid_feat, head_weight)
    dlogit = jax.nn.sigmoid(logits) - labels.astype(jnp.float32)
    feature_grad = (
        dlogit[None]
        * head_weight[:, None, None]
        * sigmoid_feat
        * (1.0 + feature * (1.0 - sigmoid_feat))
    ).astype(jnp.bfloat16)
    full_grad = lax.all_gather(feature_grad, ("date", "chan"), axis=2, tiled=True)
    temporal_part = jnp.einsum(
        "tioj,fij->tof", hidden, full_grad, preferred_element_type=jnp.float32
    )
    hidden_grad = jnp.einsum(
        "fij,tof->tioj", full_grad, temporal_weight, preferred_element_type=jnp.float32
    )
    preact_grad = (hidden_grad * sigmoid_pre * (1.0 + preact * (1.0 - sigmoid_pre))).astype(
        jnp.bfloat16
    )
    rows_out = []
    for row_off in range(3):
        cols_out = []
        for col_off in range(3):
            window = padded[:, row_off : row_off + rows, :, col_off : col_off + columns]
            cols_out.append(
                jnp.einsum("ticj,tioj->co", window, preact_grad, preferred_element_type=jnp.float32)
            )
        rows_out.append(jnp.stack(cols_out))
    spatial_part = jnp.stack(rows_out)
    grad_temporal = lax.psum(temporal_part, "pix")
    grad_spatial = lax.psum(spatial_part, ("date", "pix"))
    return (logits, grad_spatial, grad_temporal)


def solution(mesh):
    placed = (
        P(("groups", "date"), "pix", None, None),
        P(None, None, None, "chan"),
        P("chan"),
        P("date", "chan", None),
        P(),
        P(),
        P(("groups", "pix"), ("date", "chan")),
    )
    return jax.shard_map(
        shards,
        mesh=mesh,
        in_specs=placed,
        out_specs=(
            P(("groups", "pix"), ("date", "chan")),
            P("groups", None, None, "chan"),
            P("date", "chan", "groups"),
        ),
        check_vma=False,
    )
```

profile of v0, /device:TPU:0, one launch (start us, length us, event | category | flops | bytes accessed | tf_op | source)
XLA Modules:
  0.0 157.4 jit_solution(17748076628413484052)
XLA Ops:
  7.2 0.0 copy-start
  7.2 0.0 copy-start.1
  7.2 0.0 reduce-scatter.4.cloned.1.call-start
  7.2 1.1 fusion.79
  8.4 4.9 %collective-permute-start = (bf16[16,1,64,128]{3,2,1,0:T(8,128)(2,1)S(1)}, bf16[16,1,64,128]{3,2,1,0:T(8,128)(2,1)S(1)}, u32[]{:S(2)}, u32[]{:S(2)}) collective-permute-start(bf16[16,1,64,128]{3,2,1,0:T(8,128)(2,1)S(1)} %get-tuple-element.11), channel_id=1, source_target_pairs={{0,2},{1,3},{4,6},{5,7},{8,10},{9,11},{12,14},{13,15},{16,18},{17,... | collective-permute-start | bytes 786440 | tf_op jit(solution)/shard_map/ppermute | solution.py:12
  13.2 0.0 copy-start.10
  13.3 1.4 collective-permute-start.1
  14.7 1.3 fusion.47
  16.0 2.8 %collective-permute-done = bf16[16,1,64,128]{3,2,1,0:T(8,128)(2,1)S(1)} collective-permute-done((bf16[16,1,64,128]{3,2,1,0:T(8,128)(2,1)S(1)}, bf16[16,1,64,128]{3,2,1,0:T(8,128)(2,1)S(1)}, u32[]{:S(2)}, u32[]{:S(2)}) %collective-permute-start) | collective-permute-done | bytes 262176 | tf_op jit(solution)/shard_map/ppermute | solution.py:12
  18.8 4.3 %collective-permute-done.1 = bf16[16,1,64,128]{3,2,1,0:T(8,128)(2,1)S(1)} collective-permute-done((bf16[16,1,64,128]{3,2,1,0:T(8,128)(2,1)S(1)}, bf16[16,1,64,128]{3,2,1,0:T(8,128)(2,1)S(1)}, u32[]{:S(2)}, u32[]{:S(2)}) %collective-permute-start.1) | collective-permute-done | bytes 262176 | tf_op jit(solution)/shard_map/ppermute | solution.py:15
  23.0 1.1 fusion.5
  24.2 0.4 fusion.40
  24.5 0.4 fusion.51
  24.9 0.2 fusion.49
  25.1 0.2 fusion.44
  25.3 0.0 copy-start.15
  25.3 0.1 pad_maximum_fusion.1
  25.4 0.2 fusion.53
  25.6 0.2 fusion.42
  25.9 0.1 copy-done.15
  26.0 0.2 fusion.15
  26.2 0.0 copy-done.2
  26.2 1.2 multiply_convert_fusion
  27.4 0.0 copy-done
  27.4 0.2 convolution_bitcast_fusion.2
  27.6 0.8 copy.76
  28.4 1.7 %reshape.35 = f32[128,32]{1,0:T(8,128)} reshape(f32[128,2,16]{2,1,0:T(2,128)} %bitcast.179) | data formatting | bytes 32768
  30.0 0.0 reduce-scatter.4.cloned.1.call-update
  30.1 0.0 copy-start.13
  30.1 0.0 copy-start.14
  30.1 0.0 copy-start.11
  30.1 0.0 all-reduce.3.cloned.1.call-start
  30.2 2.2 %fusion.78 = (bf16[16,2,64,128]{3,2,1,0:T(8,128)(2,1)}, bf16[16,2,64,128]{3,2,1,0:T(8,128)(2,1)}, bf16[16,2,64,128]{3,2,1,0:T(8,128)(2,1)}, bf16[16,2,64,128]{3,...) fusion(bf16[16,4,64,130]{3,2,1,0:T(8,128)(2,1)S(1)} %fusion.5), kind=kLoop, calls=%fused_computation.104 | loop fusion | bytes 6291456 | tf_op jit(solution)/shard_map/slice | solution.py:29
  32.4 28.2 %reduce-scatter.4.cloned.1.call-done = f32[16,32]{1,0:T(8,128)} async-done(((f32[128,32]{1,0:T(8,128)}), f32[16,32]{1,0:T(8,128)}) %reduce-scatter.4.cloned.1.call-update) | async-done | bytes 2064
  60.6 0.8 reshape.36
  61.4 0.1 copy.77
  61.4 0.0 copy-done.13
  61.4 0.2 fusion.28
  61.6 0.0 copy-done.11
  61.7 0.1 multiply_convert_fusion.1
  61.8 0.1 copy.31
  61.9 14.0 %all_gather.3 = bf16[16,2,128]{0,1,2:T(2,128)(2,1)S(1)} all-gather(bf16[16,2,16]{0,1,2:T(2,128)(2,1)S(1)} %copy.31), channel_id=1, replica_groups=mesh['groups'=2,'date'=4,'pix'=2,'chan'=2] {'date','chan'}, dimensions={2}, use_global_device_ids=true | all-gather | bytes 9216 | tf_op jit(solution)/shard_map/all_gather | solution.py:54
  75.8 0.1 copy.32
  75.9 1.4 fusion.16
  77.3 0.3 convolution_bitcast_fusion.10
  77.6 0.3 convolution_bitcast_fusion.4
  77.9 0.0 copy-done.12
  77.9 0.0 copy-start.6
  77.9 0.3 convolution_bitcast_fusion.7
  78.2 0.2 copy-done.9
  78.4 0.3 convolution_bitcast_fusion.11
  78.6 0.0 copy-done.8
  78.6 0.3 convolution_bitcast_fusion.5
  78.9 0.3 convolution_bitcast_fusion.6
  79.2 0.3 convolution_bitcast_fusion.8
  79.4 0.3 convolution_bitcast_fusion.9
  79.7 0.1 copy-done.4
  79.8 0.3 convolution_bitcast_fusion.3
  80.1 0.7 pad_maximum_fusion.2
  80.7 0.0 all-reduce.3.cloned.1.call-update
  80.8 0.3 convolution_bitcast_fusion.1
  81.0 10.8 %psum.15 = f32[16,32,16]{1,2,0:T(8,128)} all-reduce(f32[16,32,16]{1,2,0:T(8,128)S(1)} %convolution_bitcast_fusion.1), channel_id=1, replica_groups=mesh['groups'=2,'date'=4,'pix'=2,'chan'=2] {'pix'}, use_global_device_ids=true, to_apply=%region_2.3 | all-reduce | flops 8192 | bytes 65536 | tf_op jit(solution)/shard_map/psum | solution.py:74
  91.8 57.2 %all-reduce.3.cloned.1.call-done = f32[3,3,64,32]{2,3,1,0:T(8,128)} async-done(((f32[3,3,64,32]{2,3,1,0:T(8,128)}), f32[3,3,64,32]{2,3,1,0:T(8,128)}) %all-reduce.3.cloned.1.call-update) | async-done | bytes 73744 | tf_op jit(solution)/shard_map/psum | solution.py:75
  149.0 1.6 %copy.115 = f32[3,3,64,32]{2,3,1,0:T(8,128)} copy(f32[3,3,64,32]{2,3,1,0:T(8,128)} %all-reduce.3.cloned.1.call-done) | data formatting | bytes 147456
  (18 shorter events, 0.1 us)
Async XLA Ops:
  7.2 20.3 %copy-start = (bf16[16,32,16]{1,2,0:T(8,128)(2,1)S(1)}, bf16[16,32,16]{1,2,0:T(8,128)(2,1)}, u32[]{:S(2)}) copy-start(bf16[16,32,16]{1,2,0:T(8,128)(2,1)} %param.10) | copy-start | bytes 49156
  7.2 15.9 %copy-start.1 = (bf16[16,2,64,128]{3,2,1,0:T(8,128)(2,1)S(1)}, bf16[16,2,64,128]{3,2,1,0:T(8,128)(2,1)}, u32[]{:S(2)}) copy-start(bf16[16,2,64,128]{3,2,1,0:T(8,128)(2,1)} %param.7) | copy-start | bytes 1572868
  7.2 53.4 %reduce-scatter.4.cloned.1.call-start = ((), (), s32[]{:S(2)}) async-start(), calls=%async_computation.2 | async-start | bytes 73728
  8.4 10.4 %collective-permute-start = (bf16[16,1,64,128]{3,2,1,0:T(8,128)(2,1)S(1)}, bf16[16,1,64,128]{3,2,1,0:T(8,128)(2,1)S(1)}, u32[]{:S(2)}, u32[]{:S(2)}) collective-permute-start(bf16[16,1,64,128]{3,2,1,0:T(8,128)(2,1)S(1)} %get-tuple-element.11), channel_id=1, source_target_pairs={{0,2},{1,3},{4,6},{5,7},{8,10},{9,11},{12,14},{13,15},{16,18},{17,... | collective-permute-start | bytes 786440 | tf_op jit(solution)/shard_map/ppermute | solution.py:12
  13.2 10.9 %copy-start.10 = (bf16[3,3,64,32]{2,3,1,0:T(8,128)(2,1)S(1)}, bf16[3,3,64,32]{2,3,1,0:T(8,128)(2,1)}, u32[]{:S(2)}) copy-start(bf16[3,3,64,32]{2,3,1,0:T(8,128)(2,1)} %param.8) | copy-start | bytes 110596
  13.3 9.8 %collective-permute-start.1 = (bf16[16,1,64,128]{3,2,1,0:T(8,128)(2,1)S(1)}, bf16[16,1,64,128]{3,2,1,0:T(8,128)(2,1)S(1)}, u32[]{:S(2)}, u32[]{:S(2)}) collective-permute-start(bf16[16,1,64,128]{3,2,1,0:T(8,128)(2,1)S(1)} %get-tuple-element.12), channel_id=1, source_target_pairs={{2,0},{3,1},{6,4},{7,5},{10,8},{11,9},{14,12},{15,13},{18,16},{19,... | collective-permute-start | bytes 786440 | tf_op jit(solution)/shard_map/ppermute | solution.py:15
  25.3 0.7 copy-start.15
  25.4 0.8 copy-start.2
  30.1 31.4 %copy-start.13 = (f32[16]{0:T(128)S(1)}, f32[16]{0:T(128)}, u32[]{:S(2)}) copy-start(f32[16]{0:T(128)} %param.11) | copy-start | bytes 196
  30.1 31.4 %copy-start.14 = (f32[16]{0:T(128)S(1)}, f32[16]{0:T(128)}, u32[]{:S(2)}) copy-start(f32[16]{0:T(128)} %param.12) | copy-start | bytes 196
  30.1 31.5 %copy-start.11 = (s32[2,16]{1,0:T(2,128)S(1)}, s32[2,16]{1,0:T(2,128)}, u32[]{:S(2)}) copy-start(s32[2,16]{1,0:T(2,128)} %param.13) | copy-start | bytes 388
  30.1 118.9 %all-reduce.3.cloned.1.call-start = ((), (), s32[]{:S(2)}) async-start(), calls=%async_computation.1 | async-start | bytes 294912 | tf_op jit(solution)/shard_map/psum | solution.py:75
  32.4 44.9 %copy-start.3 = (bf16[16,2,64,128]{3,2,1,0:T(8,128)(2,1)S(1)}, bf16[16,2,64,128]{3,2,1,0:T(8,128)(2,1)}, u32[]{:S(2)}) copy-start(bf16[16,2,64,128]{3,2,1,0:T(8,128)(2,1)} %copy-done.2) | copy-start | bytes 1572868
  61.6 16.2 %copy-start.12 = (f32[1,2,16]{2,0,1:T(1,128)}, f32[1,2,16]{2,0,1:T(1,128)S(1)}, u32[]{:S(2)}) copy-start(f32[1,2,16]{2,0,1:T(1,128)S(1)} %fusion.28) | copy-start | bytes 388
  77.3 1.0 copy-start.9
  77.3 1.3 copy-start.8
  77.6 1.3 copy-start.7
  77.9 1.3 copy-start.6
  78.1 1.3 copy-start.5
  78.6 1.2 copy-start.4
Sparse Core Ops, SparseCore 0:
  30.2 30.3 reduce-scatter.3
  80.9 68.0 all-reduce.2
where the time goes:
time: 158 us; the launch traced here: 157 us
  waiting for transfers between devices  92.5 us (59%)
  blocking collectives  24.7 us (16%)
  between operations  14.3 us (9%)
  local copies, waits for them, and re-layouts  8.89 us (6%)
  matrix products  8.7 us (6%)
  starting transfers between devices  6.36 us (4%)
  other arithmetic  1.98 us (1%)
    psum x1, waiting for transfers between devices, shards(): grad_spatial = lax.psum(spatial_part, ('date', 'pix'))  57.2 us
    unnamed x3, waiting for transfers between devices  28.2 us
    all_gather x1, blocking collectives, shards(): lax.all_gather(feature_grad, ('date', 'chan'), axis=2, tiled=True)  14 us
    psum x1, blocking collectives, shards(): grad_temporal = lax.psum(temporal_part, 'pix')  10.8 us
    unnamed x37, local copies, waits for them, and re-layouts  5.36 us
    ppermute x1, starting transfers between devices, with_halo(): lax.ppermute(lax.slice_in_dim(block, block.shape[dim] - width, None, axis...  4.86 us
    ppermute x1, waiting for transfers between devices, with_halo(): lax.ppermute(lax.slice_in_dim(block, 0, width, axis=dim), axis, backward)  4.27 us
    dot_general x9, matrix products, shards(): jnp.einsum('ticj,co->tioj', window, spatial_weight[row_off, col_off], pre...  4.27 us
  transfers between devices with their start and end apart: 4, of which 4 were waited for; matrix products, arithmetic and copies ran while one was open for 2% of the time, Pallas kernels for 0%

commit v1 on v0

--- a/solution.py
+++ b/solution.py
@@ -72,7 +72,7 @@
         rows_out.append(jnp.stack(cols_out))
     spatial_part = jnp.stack(rows_out)
     grad_temporal = lax.psum(temporal_part, "pix")
-    grad_spatial = lax.psum(spatial_part, ("date", "pix"))
+    grad_spatial = jnp.sum(lax.all_gather(spatial_part, ("date", "pix")), axis=0)
     return (logits, grad_spatial, grad_temporal)
 
 

time: 158 us -> 132 us (0.84)
  waiting for transfers between devices: 92.5 us -> 35.3 us
  blocking collectives: 24.7 us -> 57.3 us
  local copies, waits for them, and re-layouts: 8.89 us -> 7.05 us
    psum x1 -> x0, waiting for transfers between devices: 57.2 us -> none  [shards(): grad_spatial = lax.psum(spatial_part, ('date', 'pix'))]
    all_gather x0 -> x1, blocking collectives: none -> 33 us  [shards(): lax.all_gather(spatial_part, ('date', 'pix'))]
    unnamed x37 -> x36, local copies, waits for them, and re-layouts: 5.36 us -> 3.5 us
    unnamed x3 -> x2, waiting for transfers between devices: 28.2 us -> 28.2 us
  transfers between devices with their start and end apart: 4 -> 3, of which waited for: 4 -> 3; matrix products, arithmetic and copies ran while one was open for 2% -> 3% of each run, Pallas kernels for 0% -> 0%
where the time goes in v1:
time: 132 us; the launch traced here: 131 us
  blocking collectives  57.3 us (43%)
  waiting for transfers between devices  35.3 us (27%)
  between operations  14.3 us (11%)
  matrix products  8.79 us (7%)
  local copies, waits for them, and re-layouts  7.05 us (5%)
  starting transfers between devices  6.32 us (5%)
  other arithmetic  2.12 us (2%)
    all_gather x1, blocking collectives, shards(): lax.all_gather(spatial_part, ('date', 'pix'))  33 us
    unnamed x2, waiting for transfers between devices  28.2 us
    all_gather x1, blocking collectives, shards(): lax.all_gather(feature_grad, ('date', 'chan'), axis=2, tiled=True)  14 us
    psum x1, blocking collectives, shards(): grad_temporal = lax.psum(temporal_part, 'pix')  10.3 us
    ppermute x1, starting transfers between devices, with_halo(): lax.ppermute(lax.slice_in_dim(block, block.shape[dim] - width, None, axis...  4.86 us
    dot_general x9, matrix products, shards(): jnp.einsum('ticj,co->tioj', window, spatial_weight[row_off, col_off], pre...  4.31 us
    ppermute x1, waiting for transfers between devices, with_halo(): lax.ppermute(lax.slice_in_dim(block, 0, width, axis=dim), axis, backward)  4.27 us
    unnamed x36, local copies, waits for them, and re-layouts  3.5 us
  transfers between devices with their start and end apart: 3, of which 3 were waited for; matrix products, arithmetic and copies ran while one was open for 3% of the time, Pallas kernels for 0%

profile of v1, /device:TPU:0, one launch (start us, length us, event | category | flops | bytes accessed | tf_op | source)
XLA Modules:
  0.0 131.1 jit_solution(15926971236711038668)
XLA Ops:
  7.2 0.0 copy-start
  7.2 0.0 copy-start.1
  7.2 0.0 reduce-scatter.4.cloned.1.call-start
  7.2 1.1 fusion.79
  8.4 4.9 %collective-permute-start = (bf16[16,1,64,128]{3,2,1,0:T(8,128)(2,1)S(1)}, bf16[16,1,64,128]{3,2,1,0:T(8,128)(2,1)S(1)}, u32[]{:S(2)}, u32[]{:S(2)}) collective-permute-start(bf16[16,1,64,128]{3,2,1,0:T(8,128)(2,1)S(1)} %get-tuple-element.11), channel_id=1, source_target_pairs={{0,2},{1,3},{4,6},{5,7},{8,10},{9,11},{12,14},{13,15},{16,18},{17,... | collective-permute-start | bytes 786440 | tf_op jit(solution)/shard_map/ppermute | solution.py:12
  13.2 0.0 copy-start.10
  13.3 1.4 %collective-permute-start.1 = (bf16[16,1,64,128]{3,2,1,0:T(8,128)(2,1)S(1)}, bf16[16,1,64,128]{3,2,1,0:T(8,128)(2,1)S(1)}, u32[]{:S(2)}, u32[]{:S(2)}) collective-permute-start(bf16[16,1,64,128]{3,2,1,0:T(8,128)(2,1)S(1)} %get-tuple-element.12), channel_id=1, source_target_pairs={{2,0},{3,1},{6,4},{7,5},{10,8},{11,9},{14,12},{15,13},{18,16},{19,... | collective-permute-start | bytes 786440 | tf_op jit(solution)/shard_map/ppermute | solution.py:15
  14.7 1.3 fusion.47
  16.0 2.8 %collective-permute-done = bf16[16,1,64,128]{3,2,1,0:T(8,128)(2,1)S(1)} collective-permute-done((bf16[16,1,64,128]{3,2,1,0:T(8,128)(2,1)S(1)}, bf16[16,1,64,128]{3,2,1,0:T(8,128)(2,1)S(1)}, u32[]{:S(2)}, u32[]{:S(2)}) %collective-permute-start) | collective-permute-done | bytes 262176 | tf_op jit(solution)/shard_map/ppermute | solution.py:12
  18.8 4.3 %collective-permute-done.1 = bf16[16,1,64,128]{3,2,1,0:T(8,128)(2,1)S(1)} collective-permute-done((bf16[16,1,64,128]{3,2,1,0:T(8,128)(2,1)S(1)}, bf16[16,1,64,128]{3,2,1,0:T(8,128)(2,1)S(1)}, u32[]{:S(2)}, u32[]{:S(2)}) %collective-permute-start.1) | collective-permute-done | bytes 262176 | tf_op jit(solution)/shard_map/ppermute | solution.py:15
  23.0 0.0 copy-done.1
  23.0 1.1 fusion.5
  24.1 0.0 copy-done.10
  24.2 0.4 fusion.40
  24.5 0.4 fusion.51
  24.9 0.2 fusion.49
  25.1 0.2 fusion.44
  25.3 0.0 copy-start.15
  25.3 0.1 pad_maximum_fusion.1
  25.4 0.0 copy-start.2
  25.4 0.2 fusion.53
  25.6 0.2 fusion.42
  25.9 0.1 copy-done.15
  26.0 0.3 fusion.15
  26.2 0.0 copy-done.2
  26.2 1.2 multiply_convert_fusion
  27.5 0.0 copy-done
  27.5 0.2 convolution_bitcast_fusion.2
  27.6 0.8 copy.76
  28.4 1.7 %reshape.36 = f32[128,32]{1,0:T(8,128)} reshape(f32[128,2,16]{2,1,0:T(2,128)} %bitcast.181) | data formatting | bytes 32768
  30.1 0.0 reduce-scatter.4.cloned.1.call-update
  30.1 0.0 copy-start.13
  30.1 0.0 copy-start.14
  30.1 0.0 copy-start.11
  30.2 2.3 %fusion.78 = (bf16[16,2,64,128]{3,2,1,0:T(8,128)(2,1)}, bf16[16,2,64,128]{3,2,1,0:T(8,128)(2,1)}, bf16[16,2,64,128]{3,2,1,0:T(8,128)(2,1)}, bf16[16,2,64,128]{3,...) fusion(bf16[16,4,64,130]{3,2,1,0:T(8,128)(2,1)S(1)} %fusion.5), kind=kLoop, calls=%fused_computation.104 | loop fusion | bytes 6291456 | tf_op jit(solution)/shard_map/slice | solution.py:29
  32.4 28.2 %reduce-scatter.4.cloned.1.call-done = f32[16,32]{1,0:T(8,128)} async-done(((f32[128,32]{1,0:T(8,128)}), f32[16,32]{1,0:T(8,128)}) %reduce-scatter.4.cloned.1.call-update) | async-done | bytes 2064
  60.6 0.8 reshape.37
  61.4 0.1 copy.77
  61.5 0.0 copy-done.13
  61.5 0.0 copy-done.14
  61.5 0.2 fusion.28
  61.7 0.0 copy-done.11
  61.7 0.1 multiply_convert_fusion.1
  61.8 0.1 copy.31
  61.9 14.0 %all_gather.9 = bf16[16,2,128]{0,1,2:T(2,128)(2,1)S(1)} all-gather(bf16[16,2,16]{0,1,2:T(2,128)(2,1)S(1)} %copy.31), channel_id=1, replica_groups=mesh['groups'=2,'date'=4,'pix'=2,'chan'=2] {'date','chan'}, dimensions={2}, use_global_device_ids=true | all-gather | bytes 9216 | tf_op jit(solution)/shard_map/all_gather | solution.py:54
  75.9 0.1 copy.32
  75.9 1.4 %fusion.16 = bf16[16,2,32,128]{3,2,1,0:T(8,128)(2,1)S(1)} fusion(f32[16,2,32,128]{3,2,1,0:T(8,128)} %get-tuple-element.14, bf16[16,32,16]{1,2,0:T(8,128)(2,1)S(1)} %copy-done, bf16[16,2,128]{2,0,1:T(8,128)(2,1)S(1)} %copy.32), kind=kOutput, calls=%fused_computation.21 | convolution fusion | flops 5373952 | bytes 811008 | tf_op jit(solution)/shard_map/fij,tof->tioj/dot_general | solution.py:58
  77.3 0.0 copy-done.3
  77.4 0.0 copy-start.9
  77.4 0.0 copy-start.8
  77.4 0.3 convolution_bitcast_fusion.10
  77.6 0.3 convolution_bitcast_fusion.4
  77.9 0.3 convolution_bitcast_fusion.1
  78.2 0.3 convolution_bitcast_fusion.7
  78.5 10.3 %psum.7 = f32[16,32,16]{1,2,0:T(8,128)} all-reduce(f32[16,32,16]{1,2,0:T(8,128)S(1)} %convolution_bitcast_fusion.1), channel_id=1, replica_groups=mesh['groups'=2,'date'=4,'pix'=2,'chan'=2] {'pix'}, use_global_device_ids=true, to_apply=%region_2.3 | all-reduce | flops 8192 | bytes 65536 | tf_op jit(solution)/shard_map/psum | solution.py:74
  88.8 0.3 convolution_bitcast_fusion.11
  89.1 0.0 copy-done.8
  89.1 0.3 convolution_bitcast_fusion.5
  89.3 0.3 convolution_bitcast_fusion.6
  89.6 0.3 convolution_bitcast_fusion.8
  89.9 0.3 convolution_bitcast_fusion.9
  90.2 0.3 convolution_bitcast_fusion.3
  90.5 33.0 %all-gather = f32[24,3,64,32]{2,3,1,0:T(8,128)S(1)} all-gather(f32[3,3,64,32]{2,3,1,0:T(8,128)S(1)} %pad_maximum_fusion.2), channel_id=2, replica_groups=mesh['groups'=2,'date'=4,'pix'=2,'chan'=2] {'date','pix'}, dimensions={0}, use_global_device_ids=true | all-gather | bytes 663552 | tf_op jit(solution)/shard_map/all_gather | solution.py:75
  123.5 0.8 reduce_sum.9
  (16 shorter events, 0.1 us)
Async XLA Ops:
  7.2 20.3 %copy-start = (bf16[16,32,16]{1,2,0:T(8,128)(2,1)S(1)}, bf16[16,32,16]{1,2,0:T(8,128)(2,1)}, u32[]{:S(2)}) copy-start(bf16[16,32,16]{1,2,0:T(8,128)(2,1)} %param.10) | copy-start | bytes 49156
  7.2 15.9 %copy-start.1 = (bf16[16,2,64,128]{3,2,1,0:T(8,128)(2,1)S(1)}, bf16[16,2,64,128]{3,2,1,0:T(8,128)(2,1)}, u32[]{:S(2)}) copy-start(bf16[16,2,64,128]{3,2,1,0:T(8,128)(2,1)} %param.7) | copy-start | bytes 1572868
  7.2 53.4 %reduce-scatter.4.cloned.1.call-start = ((), (), s32[]{:S(2)}) async-start(), calls=%async_computation.1 | async-start | bytes 73728
  8.4 10.4 %collective-permute-start = (bf16[16,1,64,128]{3,2,1,0:T(8,128)(2,1)S(1)}, bf16[16,1,64,128]{3,2,1,0:T(8,128)(2,1)S(1)}, u32[]{:S(2)}, u32[]{:S(2)}) collective-permute-start(bf16[16,1,64,128]{3,2,1,0:T(8,128)(2,1)S(1)} %get-tuple-element.11), channel_id=1, source_target_pairs={{0,2},{1,3},{4,6},{5,7},{8,10},{9,11},{12,14},{13,15},{16,18},{17,... | collective-permute-start | bytes 786440 | tf_op jit(solution)/shard_map/ppermute | solution.py:12
  13.2 10.9 %copy-start.10 = (bf16[3,3,64,32]{2,3,1,0:T(8,128)(2,1)S(1)}, bf16[3,3,64,32]{2,3,1,0:T(8,128)(2,1)}, u32[]{:S(2)}) copy-start(bf16[3,3,64,32]{2,3,1,0:T(8,128)(2,1)} %param.8) | copy-start | bytes 110596
  13.3 9.8 %collective-permute-start.1 = (bf16[16,1,64,128]{3,2,1,0:T(8,128)(2,1)S(1)}, bf16[16,1,64,128]{3,2,1,0:T(8,128)(2,1)S(1)}, u32[]{:S(2)}, u32[]{:S(2)}) collective-permute-start(bf16[16,1,64,128]{3,2,1,0:T(8,128)(2,1)S(1)} %get-tuple-element.12), channel_id=1, source_target_pairs={{2,0},{3,1},{6,4},{7,5},{10,8},{11,9},{14,12},{15,13},{18,16},{19,... | collective-permute-start | bytes 786440 | tf_op jit(solution)/shard_map/ppermute | solution.py:15
  25.3 0.7 copy-start.15
  25.4 0.8 copy-start.2
  30.1 31.4 %copy-start.13 = (f32[16]{0:T(128)S(1)}, f32[16]{0:T(128)}, u32[]{:S(2)}) copy-start(f32[16]{0:T(128)} %param.11) | copy-start | bytes 196
  30.1 31.4 %copy-start.14 = (f32[16]{0:T(128)S(1)}, f32[16]{0:T(128)}, u32[]{:S(2)}) copy-start(f32[16]{0:T(128)} %param.12) | copy-start | bytes 196
  30.1 31.5 %copy-start.11 = (s32[2,16]{1,0:T(2,128)S(1)}, s32[2,16]{1,0:T(2,128)}, u32[]{:S(2)}) copy-start(s32[2,16]{1,0:T(2,128)} %param.13) | copy-start | bytes 388
  32.4 44.9 %copy-start.3 = (bf16[16,2,64,128]{3,2,1,0:T(8,128)(2,1)S(1)}, bf16[16,2,64,128]{3,2,1,0:T(8,128)(2,1)}, u32[]{:S(2)}) copy-start(bf16[16,2,64,128]{3,2,1,0:T(8,128)(2,1)} %copy-done.2) | copy-start | bytes 1572868
  61.7 16.2 %copy-start.12 = (f32[1,2,16]{2,0,1:T(1,128)}, f32[1,2,16]{2,0,1:T(1,128)S(1)}, u32[]{:S(2)}) copy-start(f32[1,2,16]{2,0,1:T(1,128)S(1)} %fusion.28) | copy-start | bytes 388
  77.4 11.4 %copy-start.9 = (bf16[16,2,64,128]{3,2,1,0:T(8,128)(2,1)S(1)}, bf16[16,2,64,128]{3,2,1,0:T(8,128)(2,1)}, u32[]{:S(2)}) copy-start(bf16[16,2,64,128]{3,2,1,0:T(8,128)(2,1)} %get-tuple-element.3) | copy-start | bytes 1572868
  77.4 11.7 %copy-start.8 = (bf16[16,2,64,128]{3,2,1,0:T(8,128)(2,1)S(1)}, bf16[16,2,64,128]{3,2,1,0:T(8,128)(2,1)}, u32[]{:S(2)}) copy-start(bf16[16,2,64,128]{3,2,1,0:T(8,128)(2,1)} %get-tuple-element.4) | copy-start | bytes 1572868
  77.6 11.7 %copy-start.7 = (bf16[16,2,64,128]{3,2,1,0:T(8,128)(2,1)S(1)}, bf16[16,2,64,128]{3,2,1,0:T(8,128)(2,1)}, u32[]{:S(2)}) copy-start(bf16[16,2,64,128]{3,2,1,0:T(8,128)(2,1)} %get-tuple-element.5) | copy-start | bytes 1572868
  78.2 11.4 %copy-start.6 = (bf16[16,2,64,128]{3,2,1,0:T(8,128)(2,1)S(1)}, bf16[16,2,64,128]{3,2,1,0:T(8,128)(2,1)}, u32[]{:S(2)}) copy-start(bf16[16,2,64,128]{3,2,1,0:T(8,128)(2,1)} %get-tuple-element.6) | copy-start | bytes 1572868
  78.5 11.4 %copy-start.5 = (bf16[16,2,64,128]{3,2,1,0:T(8,128)(2,1)S(1)}, bf16[16,2,64,128]{3,2,1,0:T(8,128)(2,1)}, u32[]{:S(2)}) copy-start(bf16[16,2,64,128]{3,2,1,0:T(8,128)(2,1)} %get-tuple-element.7) | copy-start | bytes 1572868
  89.1 1.1 copy-start.4
Sparse Core Ops, SparseCore 0:
  30.2 30.3 reduce-scatter.3
